TPU v7x, 32 devices: a whole 2x2x4 slice. The times are simulated.
32 devices in a mesh: groups: 2 (over y), replica: 2 (over core), tensor: 8 (over z, x).
Axes of the slice: x: 2, y: 2, z: 4, core: 2. Of those that a mesh axis runs over, the one named last changes fastest.
Arguments:
- query: bfloat16 [32, 8192], P(('groups', 'replica'), 'tensor'), parts along dimension 0, may hold values from -120 to 120
- key_cache_rows: bfloat16 [32, 8, 256, 128], P(('groups', 'replica'), None, 'tensor'), parts along dimension 0, may hold values from -6 to 6
- value_cache_rows: bfloat16 [32, 8, 256, 128], P(('groups', 'replica'), None, 'tensor'), parts along dimension 0, may hold values from -48 to 48
- cache_length: int32 [32], P(('groups', 'replica')), parts along dimension 0, may hold values from 2 to 256
- output_weight: bfloat16 [8192, 8192], P('tensor'), may hold values from -0.0625 to 0.0625
- adapter_down_weight: bfloat16 [256, 64, 8192], P('replica', None, 'tensor'), may hold values from -0.0625 to 0.0625
- adapter_up_weight: bfloat16 [256, 64, 8192], P('replica', None, 'tensor'), may hold values from -0.75 to 0.75
- slot_adapter_table: int32 [64], P('groups'), parts along dimension 0, may hold values from 0 to 255, as said below
- request_slot: int32 [32], P(('groups', 'replica')), parts along dimension 0, may hold values from 0 to 15
Outputs:
- mixed: bfloat16 [32, 8192], P(('groups', 'replica'), 'tensor'), parts along dimension 0
There are 2 independent parts, one for each index of `groups`. A program takes and returns all parts, laid end to end along the dimension named above; an argument that names none is the same for every part. Nothing has to cross between parts.
Inputs may be any that keep to these rules, and one draw needn't show every extreme that they name: `slot_adapter_table`: the 16 adapters of one replica's slots are distinct.
All inputs are finite; a program needn't handle non-finite values.
Results may differ from a plain program's by a relative error of at most 0.015.
Values may be sent and summed in bfloat16 or wider, within the bound.
A program may use at most 192 MiB of HBM per device.

v0:
```python
import jax
import jax.numpy as jnp
from jax import lax
from jax.sharding import PartitionSpec as P

QUERY_HEADS = 64
KVH = 8
SLOTS = 16


def shards(
    query,
    key_cache_rows,
    value_cache_rows,
    cache_length,
    output_weight,
    adapter_down_weight,
    adapter_up_weight,
    slot_adapter_table,
    request_slot,
):
    n_tensor = lax.axis_size("tensor")
    t_index = lax.axis_index("tensor")
    r_index = lax.axis_index("replica")
    n_replica = lax.axis_size("replica")
    requests = query.shape[0]
    span = key_cache_rows.shape[2]
    head_size = key_cache_rows.shape[3]
    group = QUERY_HEADS // KVH
    own_heads = QUERY_HEADS // n_tensor
    whole = lax.all_gather(query, "tensor", axis=1, tiled=True)
    heads = whole.reshape(requests, KVH, group, head_size)
    score = jnp.einsum("tkgd,tkcd->tkgc", heads, key_cache_rows, preferred_element_type=jnp.float32)
    score = score / jnp.sqrt(jnp.float32(head_size))
    positions = t_index * span + jnp.arange(span, dtype=jnp.int32)
    live = (positions[None, :] < cache_length[:, None])[:, None, None, :]
    masked = jnp.where(live, score, jnp.float32(-1e30))
    rough_top = lax.optimization_barrier(jnp.max(masked, axis=3).astype(jnp.bfloat16))
    top = rough_top.astype(jnp.float32)
    expo = jnp.where(live, jnp.exp(masked - top[..., None]), jnp.float32(0.0))
    total = jnp.sum(expo, axis=3)
    summed = jnp.einsum(
        "tkgc,tkcd->tkgd",
        expo.astype(jnp.bfloat16),
        value_cache_rows,
        preferred_element_type=jnp.float32,
    )
    top = top.reshape(requests, QUERY_HEADS)
    total = total.reshape(requests, QUERY_HEADS)
    summed = summed.reshape(requests, QUERY_HEADS, head_size)
    received = (
        lax.all_to_all(
            top[None].astype(jnp.bfloat16), "tensor", split_axis=2, concat_axis=0, tiled=True
        ).astype(jnp.float32),
        lax.all_to_all(
            total[None].astype(jnp.bfloat16), "tensor", split_axis=2, concat_axis=0, tiled=True
        ).astype(jnp.float32),
        lax.all_to_all(
            summed[None].astype(jnp.bfloat16), "tensor", split_axis=2, concat_axis=0, tiled=True
        ).astype(jnp.float32),
    )
    peak = jnp.max(received[0], axis=0)
    factor = jnp.exp(received[0] - peak[None])
    whole_total = jnp.sum(received[1] * factor, axis=0)
    whole_sum = jnp.sum(received[2] * factor[..., None], axis=0)
    result = whole_sum / whole_total[..., None]
    attention_output = result.reshape(result.shape[0], own_heads * head_size).astype(jnp.bfloat16)
    partial_value = jnp.dot(attention_output, output_weight, preferred_element_type=jnp.float32)
    base = lax.psum_scatter(partial_value, "tensor", scatter_dimension=1, tiled=True)
    resident_count = adapter_down_weight.shape[0]
    table = slot_adapter_table.reshape(n_replica, SLOTS)
    is_resident = table // resident_count == r_index
    replica_slot_index = table % resident_count
    rank_position = adapter_down_weight.shape[1]
    picks = request_slot[:, None] == jnp.arange(SLOTS, dtype=jnp.int32)[None, :]
    send_down = jnp.where(
        is_resident[:, :, None, None],
        adapter_down_weight[replica_slot_index],
        jnp.zeros((), jnp.bfloat16),
    )
    forward_up_rows = jnp.where(
        is_resident[:, :, None, None],
        adapter_up_weight[replica_slot_index],
        jnp.zeros((), jnp.bfloat16),
    )
    got_down, got_up = (
        lax.all_to_all(send_down, "replica", split_axis=0, concat_axis=0, tiled=True),
        lax.all_to_all(forward_up_rows, "replica", split_axis=0, concat_axis=0, tiled=True),
    )
    slot_down = jnp.sum(got_down.astype(jnp.float32), axis=0).astype(jnp.bfloat16)
    slot_up = jnp.sum(got_up.astype(jnp.float32), axis=0).astype(jnp.bfloat16)
    every_slot = jnp.einsum(
        "tf,srf->tsr", attention_output, slot_down, preferred_element_type=jnp.float32
    )
    shrink_part = jnp.sum(jnp.where(picks[:, :, None], every_slot, jnp.float32(0.0)), axis=1)
    reduced_features = lax.psum(shrink_part, "tensor").astype(jnp.bfloat16)
    placed = jnp.where(picks[:, :, None], reduced_features[:, None, :], jnp.zeros((), jnp.bfloat16))
    expand = jnp.dot(
        placed.reshape(requests, SLOTS * rank_position),
        slot_up.reshape(SLOTS * rank_position, slot_up.shape[2]),
        preferred_element_type=jnp.float32,
    )
    return (base + expand).astype(jnp.bfloat16)


def solution(mesh):
    in_specs = (
        P(("groups", "replica"), "tensor"),
        P(("groups", "replica"), None, "tensor", None),
        P(("groups", "replica"), None, "tensor", None),
        P(("groups", "replica")),
        P("tensor", None),
        P("replica", None, "tensor"),
        P("replica", None, "tensor"),
        P("groups"),
        P(("groups", "replica")),
    )
    out_specs = P(("groups", "replica"), "tensor")
    return jax.shard_map(shards, mesh=mesh, in_specs=in_specs, out_specs=out_specs, check_vma=False)
```

profile of v0, /device:TPU:0, one launch (start us, length us, event | category | flops | bytes accessed | tf_op | source)
XLA Modules:
  0.0 165.8 jit_solution(8116217600831578496)
XLA Ops:
  6.5 32.6 %all_gather.3 = bf16[8,8192]{1,0:T(8,128)(2,1)S(1)} all-gather(bf16[8,1024]{1,0:T(8,128)(2,1)} %param.9), channel_id=1, replica_groups=mesh['groups'=2,'replica'=2,'tensor'=8] {'tensor'}, dimensions={1}, use_global_device_ids=true | all-gather | bytes 147456 | tf_op jit(solution)/shard_map/all_gather | solution.py:31
  39.2 0.7 broadcast_compare_fusion
  39.9 1.5 fusion.27
  41.5 0.7 copy.26
  42.2 5.5 %all-to-all-start.1 = ((bf16[1,8,64]{1,0,2:T(2,128)(2,1)}), bf16[1,8,64]{1,0,2:T(2,128)(2,1)S(1)}, u32[]{:S(2)}, u32[]{:S(2)}) async-start(bf16[1,8,64]{1,0,2:T(2,128)(2,1)} %copy.26), calls=%async_computation.1 | async-start | bytes 65536 | tf_op jit(solution)/shard_map/all_to_all | solution.py:52
  47.7 0.7 reshape.217
  48.4 0.7 reshape.216
  50.7 3.7 %all-to-all-done.1 = bf16[1,8,64]{1,0,2:T(2,128)(2,1)S(1)} async-done(((bf16[1,8,64]{1,0,2:T(2,128)(2,1)}), bf16[1,8,64]{1,0,2:T(2,128)(2,1)S(1)}, u32[]{:S(2)}, u32[]{:S(2)}) %all-to-all-start.1) | async-done | bytes 1056 | tf_op jit(solution)/shard_map/all_to_all | solution.py:52
  54.4 3.3 %all-to-all-start.2 = ((bf16[1,8,64]{1,0,2:T(2,128)(2,1)}), bf16[1,8,64]{1,0,2:T(2,128)(2,1)S(1)}, u32[]{:S(2)}, u32[]{:S(2)}) async-start(bf16[1,8,64]{1,0,2:T(2,128)(2,1)} %copy.29), calls=%async_computation.2 | async-start | bytes 65536 | tf_op jit(solution)/shard_map/all_to_all | solution.py:55
  57.7 0.7 copy.25
  58.5 8.5 %gather_fusion = bf16[32,64,1024]{2,1,0:T(8,128)(2,1)} fusion(bf16[128,64,1024]{2,1,0:T(8,128)(2,1)} %param.14, s32[1024]{0:T(1024)S(1)} %pad_clamp_fusion), kind=kCustom, calls=%fused_computation | custom fusion | bytes 8388736 | tf_op jit(solution)/shard_map/gather | solution.py:78
  67.0 8.6 %gather_fusion.1 = bf16[32,64,1024]{2,1,0:T(8,128)(2,1)} fusion(bf16[128,64,1024]{2,1,0:T(8,128)(2,1)} %param.15, s32[1024]{0:T(1024)S(1)} %pad_clamp_fusion), kind=kCustom, calls=%fused_computation.1 | custom fusion | bytes 8388736 | tf_op jit(solution)/shard_map/gather | solution.py:83
  75.7 5.9 %all-to-all-start = ((bf16[1,8,64,128]{3,1,0,2:T(8,128)(2,1)}), bf16[1,8,64,128]{3,1,0,2:T(8,128)(2,1)S(1)}, u32[]{:S(2)}, u32[]{:S(2)}) async-start(bf16[1,8,64,128]{3,1,0,2:T(8,128)(2,1)} %copy.25), calls=%async_computation | async-start | bytes 262144 | tf_op jit(solution)/shard_map/all_to_all | solution.py:58
  82.1 6.9 %all-to-all-done = bf16[1,8,64,128]{3,1,0,2:T(8,128)(2,1)S(1)} async-done(((bf16[1,8,64,128]{3,1,0,2:T(8,128)(2,1)}), bf16[1,8,64,128]{3,1,0,2:T(8,128)(2,1)S(1)}, u32[]{:S(2)}, u32[]{:S(2)}) %all-to-all-start) | async-done | bytes 131104 | tf_op jit(solution)/shard_map/all_to_all | solution.py:58
  89.1 8.8 %fusion.19 = f32[8,8192]{1,0:T(8,128)} fusion(bf16[1024,8192]{1,0:T(8,128)(2,1)} %param.13, f32[8,8,128]{2,0,1:T(8,128)S(1)} %fusion.5, f32[8,8]{0,1:T(8,128)S(1)} %copy.31), kind=kOutput, calls=%fused_computation.31 | convolution fusion | flops 134234112 | bytes 17072384 | tf_op jit(solution)/shard_map/dot_general | solution.py:68
  97.9 5.1 %broadcast_select_fusion.1 = (bf16[2,16,64,1024]{3,2,1,0:T(8,128)(2,1)S(1)}, bf16[2,16,64,1024]{3,2,1,0:T(8,128)(2,1)}) fusion(bf16[2,16,64,1024]{3,2,1,0:T(8,128)(2,1)} %bitcast.53, pred[2,16]{1,0:T(4,128)(4,1)S(1)} %fusion.24, bf16[2,16,64,1024]{3,2,1,0:T(8,128)(2,1)} %bitcast.54), kind=kLoop, calls=%fused_computation.3 | loop fusion | flops 4194304 | bytes 16777248 | tf_op jit(solution)/shard_map/jit(_where)/select_n | solution.py:76
  103.1 8.1 %all_to_all.43 = bf16[2,16,64,1024]{3,2,1,0:T(8,128)(2,1)} all-to-all(bf16[2,16,64,1024]{3,2,1,0:T(8,128)(2,1)S(1)} %get-tuple-element.7), channel_id=1, replica_groups=mesh['groups'=2,'replica'=2,'tensor'=8] {'replica'}, dimensions={0} | all-to-all | bytes 8388608 | tf_op jit(solution)/shard_map/all_to_all | solution.py:87
  111.2 5.6 %all-to-all-start.4 = ((bf16[2,16,64,1024]{3,2,1,0:T(8,128)(2,1)}), bf16[2,16,64,1024]{3,2,1,0:T(8,128)(2,1)}, u32[]{:S(2)}, u32[]{:S(2)}) async-start(bf16[2,16,64,1024]{3,2,1,0:T(8,128)(2,1)} %get-tuple-element.8), calls=%async_computation.5 | async-start | bytes 8388608 | tf_op jit(solution)/shard_map/all_to_all | solution.py:88
  116.9 5.3 %reduce_sum.63 = bf16[16,64,1024]{2,1,0:T(8,128)(2,1)} reduce(bf16[2,16,64,1024]{3,2,1,0:T(8,128)(2,1)} %all_to_all.43, bf16[]{:T(256)} %constant.55.clone.1), dimensions={0}, to_apply=%region_6.7 | reduce | flops 1048576 | bytes 6291458 | tf_op jit(solution)/shard_map/reduce_sum | solution.py:90
  122.1 3.7 %reduce_sum.65 = bf16[16,64,1024]{2,1,0:T(8,128)(2,1)S(1)} reduce(bf16[2,16,64,1024]{3,2,1,0:T(8,128)(2,1)} %all-to-all-done.4, bf16[]{:T(256)} %constant.55.clone.1), dimensions={0}, to_apply=%region_9.10 | reduce | flops 1048576 | bytes 6291458 | tf_op jit(solution)/shard_map/reduce_sum | solution.py:91
  125.8 2.5 %fusion.2 = f32[8,64]{1,0:T(8,128)S(1)} fusion(bf16[16,64,1024]{2,1,0:T(8,128)(2,1)} %reduce_sum.63, pred[8,16]{0,1:T(8,128)(4,1)S(1)} %iota_compare_fusion, f32[8,8,128]{2,0,1:T(8,128)S(1)} %fusion.5, f32[8,8]{0,1:T(8,128)S(1)} %copy.31), kind=kOutput, calls=%fused_computation.9 | convolution fusion | flops 16809472 | bytes 2132352 | tf_op jit(solution)/shard_map/tf,srf->tsr/dot_general | solution.py:92
  128.4 18.2 %psum.7 = bf16[8,64]{1,0:T(8,128)(2,1)S(1)} all-reduce(f32[8,64]{1,0:T(8,128)S(1)} %fusion.2), channel_id=1, replica_groups=mesh['groups'=2,'replica'=2,'tensor'=8] {'tensor'}, use_global_device_ids=true, to_apply=%region_8.9 | all-reduce | flops 512 | bytes 3072 | tf_op jit(solution)/shard_map/psum | solution.py:96
  146.6 10.5 %reduce-scatter.2.cloned.1.call-done = f32[8,1024]{1,0:T(8,128)} async-done(((f32[8,8192]{1,0:T(8,128)}), f32[8,1024]{1,0:T(8,128)}) %reduce-scatter.2.cloned.1.call-update) | async-done | bytes 32784 | tf_op jit(solution)/shard_map/reduce_scatter | solution.py:69
  157.1 1.9 %fusion.4 = bf16[8,1024]{1,0:T(8,128)(2,1)} fusion(f32[8,1024]{1,0:T(8,128)} %reduce-scatter.2.cloned.1.call-done, bf16[16,64,1024]{2,1,0:T(8,128)(2,1)S(1)} %reduce_sum.65, pred[8,16]{0,1:T(8,128)(4,1)S(1)} %iota_compare_fusion, bf16[8,64]{1,0:T(8,128)(2,1)S(1)} %psum.7), kind=kOutput, calls=%fused_computation.12 | convolution fusion | flops 16801792 | bytes 2147456 | tf_op jit(solution)/shard_map/dot_general | solution.py:98
  (32 shorter events, 2.4 us)
Async XLA Ops:
  6.5 42.7 %copy-start = (bf16[8,8,32,128]{3,2,1,0:T(8,128)(2,1)S(1)}, bf16[8,8,32,128]{3,2,1,0:T(8,128)(2,1)}, u32[]{:S(2)}) copy-start(bf16[8,8,32,128]{3,2,1,0:T(8,128)(2,1)} %param.11) | copy-start | bytes 1572868
  42.2 12.1 %all-to-all-start.1 = ((bf16[1,8,64]{1,0,2:T(2,128)(2,1)}), bf16[1,8,64]{1,0,2:T(2,128)(2,1)S(1)}, u32[]{:S(2)}, u32[]{:S(2)}) async-start(bf16[1,8,64]{1,0,2:T(2,128)(2,1)} %copy.26), calls=%async_computation.1 | async-start | bytes 65536 | tf_op jit(solution)/shard_map/all_to_all | solution.py:52
  54.4 21.3 %all-to-all-start.2 = ((bf16[1,8,64]{1,0,2:T(2,128)(2,1)}), bf16[1,8,64]{1,0,2:T(2,128)(2,1)S(1)}, u32[]{:S(2)}, u32[]{:S(2)}) async-start(bf16[1,8,64]{1,0,2:T(2,128)(2,1)} %copy.29), calls=%async_computation.2 | async-start | bytes 65536 | tf_op jit(solution)/shard_map/all_to_all | solution.py:55
  75.7 13.3 %all-to-all-start = ((bf16[1,8,64,128]{3,1,0,2:T(8,128)(2,1)}), bf16[1,8,64,128]{3,1,0,2:T(8,128)(2,1)S(1)}, u32[]{:S(2)}, u32[]{:S(2)}) async-start(bf16[1,8,64,128]{3,1,0,2:T(8,128)(2,1)} %copy.25), calls=%async_computation | async-start | bytes 262144 | tf_op jit(solution)/shard_map/all_to_all | solution.py:58
  81.6 75.5 %reduce-scatter.2.cloned.1.call-start = ((), (), s32[]{:S(2)}) async-start(), calls=%async_computation.6 | async-start | bytes 294912 | tf_op jit(solution)/shard_map/reduce_scatter | solution.py:69
  111.2 10.9 %all-to-all-start.4 = ((bf16[2,16,64,1024]{3,2,1,0:T(8,128)(2,1)}), bf16[2,16,64,1024]{3,2,1,0:T(8,128)(2,1)}, u32[]{:S(2)}, u32[]{:S(2)}) async-start(bf16[2,16,64,1024]{3,2,1,0:T(8,128)(2,1)} %get-tuple-element.8), calls=%async_computation.5 | async-start | bytes 8388608 | tf_op jit(solution)/shard_map/all_to_all | solution.py:88
  116.8 42.1 %copy-start.1 = (bf16[8,8,32,128]{3,2,1,0:T(8,128)(2,1)S(1)}, bf16[8,8,32,128]{3,2,1,0:T(8,128)(2,1)}, u32[]{:S(2)}) copy-start(bf16[8,8,32,128]{3,2,1,0:T(8,128)(2,1)} %param.11) | copy-start | bytes 1572868
  122.1 3.7 %copy-start.2 = (s32[8]{0:T(128)S(1)}, s32[8]{0:T(128)}, u32[]{:S(2)}) copy-start(s32[8]{0:T(128)} %param.17) | copy-start | bytes 100
Sparse Core Ops, SparseCore 0:
  98.1 59.0 reduce-scatter.1
where the time goes:
time: 167 us; the launch traced here: 166 us
  blocking collectives  59 us (35%)
  local copies, waits for them, and re-layouts  21.5 us (13%)
  waiting for transfers between devices  21.1 us (13%)
  starting transfers between devices  20.4 us (12%)
  other arithmetic  15.3 us (9%)
  matrix products  15 us (9%)
  between operations  13.5 us (8%)
    all_gather x1, blocking collectives, shards(): whole = lax.all_gather(query, 'tensor', axis=1, tiled=True)  32.6 us
    psum x1, blocking collectives, shards(): reduced_features = lax.psum(shrink_part, 'tensor').astype(jnp.bfloat16)  18.2 us
    reduce_scatter x1, waiting for transfers between devices, shards(): lax.psum_scatter(partial_value, 'tensor', scatter_dimension=1, tiled=True)  10.5 us
    dot_general x1, matrix products, shards(): jnp.dot(attention_output, output_weight, preferred_element_type=jnp.float32)  8.8 us
    gather x1, local copies, waits for them, and re-layouts, shards(): adapter_up_weight[replica_slot_index]  8.55 us
    gather x1, local copies, waits for them, and re-layouts, shards(): adapter_down_weight[replica_slot_index]  8.51 us
    all_to_all x1, blocking collectives, shards(): lax.all_to_all(send_down, 'replica', split_axis=0, concat_axis=0, tiled=T...  8.14 us
    all_to_all x1, waiting for transfers between devices, shards(): lax.all_to_all(summed[None].astype(jnp.bfloat16), 'tensor', split_axis=2,...  6.93 us
  transfers between devices with their start and end apart: 5, of which 3 were waited for; matrix products, arithmetic and copies ran while one was open for 23% of the time, Pallas kernels for 0%

commit v1 on v0

v1 whole, which is shorter than its diff:
```python
import functools

import jax
import jax.numpy as jnp
from jax import lax
from jax.experimental import pallas as pl
from jax.experimental.pallas import tpu as pltpu
from jax.sharding import PartitionSpec as P

QUERY_HEADS = 64
F32, BF16 = jnp.float32, jnp.bfloat16
MESH = pl.DeviceIdType.MESH


def repeat(lo, hi, body):
    if hi - lo <= 8:
        for i in range(lo, hi):
            body(i)
    else:
        lax.fori_loop(lo, hi, lambda i, c: (body(i), c)[1], 0)


def gather_kernel(table, down, up, out_down, out_up, sems):
    resident = down.shape[0]
    copies = []
    for s in range(out_down.shape[0]):
        index = lax.rem(table[s], resident)
        copies.append(pltpu.make_async_copy(down.at[index], out_down.at[s], sems.at[0, s]))
        copies.append(pltpu.make_async_copy(up.at[index], out_up.at[s], sems.at[1, s]))
    for c in copies:
        c.start()
    for c in copies:
        c.wait()


def main_kernel(
    n, resident,
    length, slot, table, query, key_hbm, value_hbm, weight_hbm, down_hbm, up_hbm,
    out,
    key, value, weight, down, up,
    q_send, q_all, pay_send, pay_all, att_send, att_recv, code_send, code_recv,
    shr_send, shr_all, base_send, base_all, fin_own, fin_send, fin_recv,
    load_sem, w_sem, q_ss, q_rs, pay_ss, pay_rs, shr_ss, shr_rs, base_ss, base_rs, pair_ss, pair_rs,
):
    me = lax.axis_index("tensor")
    r = lax.axis_index("replica")
    requests, features = query.shape
    head = key.shape[3]
    kv_heads, span = key.shape[1], key.shape[2]
    own = features // head
    group = QUERY_HEADS // kv_heads
    rows = q_send.shape[0]
    width = weight.shape[2]
    split = width < features
    slots = down.shape[0]
    rank = down.shape[1]

    def peer(i):
        return lax.rem(me + i, n)

    def w_copy(i):
        p = peer(i)
        start = p * features + (r * width if split else 0)
        return pltpu.make_async_copy(
            weight_hbm.at[:, pl.ds(pl.multiple_of(start, 128), width)], weight.at[i % n], w_sem.at[i % n]
        )

    loads = [
        pltpu.make_async_copy(key_hbm, key, load_sem.at[0]),
        pltpu.make_async_copy(value_hbm, value, load_sem.at[1]),
        pltpu.make_async_copy(down_hbm, down, load_sem.at[2]),
        pltpu.make_async_copy(up_hbm, up, load_sem.at[3]),
    ]
    for c in loads[:3]:
        c.start()
    repeat(1, n + 1, lambda i: w_copy(i).start())
    loads[3].start()

    barrier = pltpu.get_barrier_semaphore()
    repeat(1, n, lambda i: pl.semaphore_signal(barrier, inc=1, device_id={"tensor": peer(i)}, device_id_type=MESH))
    pl.semaphore_signal(barrier, inc=1, device_id={"replica": 1 - r}, device_id_type=MESH)

    q = query[...].astype(F32)
    pieces = [q[:, h * head : (h + 1) * head] for h in range(own)]
    while len(pieces) * requests < rows:
        pieces.append(jnp.zeros_like(pieces[0]))
    q_send[...] = jnp.concatenate(pieces, axis=0).astype(BF16)

    row_of = lax.broadcasted_iota(jnp.int32, (requests, 128), 0)
    code_own = jnp.full((requests, 128), -1, jnp.int32)
    code_other = jnp.full((requests, 128), -1, jnp.int32)
    for t in range(requests):
        placed = r * (slots // 2) + slot[t]
        home = table[placed] // resident
        code_own = jnp.where(row_of == t, jnp.where(home == r, placed, -1), code_own)
        code_other = jnp.where(row_of == t, jnp.where(home == r, -1, placed), code_other)
    code_send[...] = code_other

    pl.semaphore_wait(barrier, n)

    def to_peer(src, dst, ss, rs, i):
        return pltpu.make_async_remote_copy(
            src_ref=src, dst_ref=dst.at[me], send_sem=ss.at[i], recv_sem=rs.at[me],
            device_id={"tensor": peer(i)}, device_id_type=MESH,
        )

    def from_peer(src, dst, ss, rs, i):
        p = peer(i)
        return pltpu.make_async_remote_copy(
            src_ref=src, dst_ref=dst.at[p], send_sem=ss.at[i], recv_sem=rs.at[p],
            device_id={"tensor": p}, device_id_type=MESH,
        )

    def to_pair(src, dst, k):
        return pltpu.make_async_remote_copy(
            src_ref=src, dst_ref=dst, send_sem=pair_ss.at[k], recv_sem=pair_rs.at[k],
            device_id={"replica": 1 - r}, device_id_type=MESH,
        )

    repeat(1, n, lambda i: to_peer(q_send, q_all, q_ss, q_rs, i).start())
    codes = to_pair(code_send, code_recv, 0)
    codes.start()

    columns = requests * span
    col = lax.broadcasted_iota(jnp.int32, (rows, columns), 1)
    row = lax.broadcasted_iota(jnp.int32, (rows, columns), 0)
    limit = jnp.zeros((rows, columns), jnp.int32)
    for t in range(requests):
        limit = jnp.where(col // span == t, length[t], limit)
    live = (lax.rem(row, requests) == col // span) & (me * span + lax.rem(col, span) < limit)
    eye = lax.broadcasted_iota(jnp.int32, (rows, 128), 0) == lax.broadcasted_iota(jnp.int32, (rows, 128), 1)
    stat_row = lax.broadcasted_iota(jnp.int32, (16, 128), 0)
    scale = 1.0 / (float(head) ** 0.5)

    loads[0].wait()
    loads[1].wait()

    def as_row(c):
        return jnp.sum(jnp.where(eye, c, 0.0), axis=0, keepdims=True)

    def attend(p, q_rows):
        kv = (p * own) // group
        k = key[:, kv].reshape(columns, head)
        v = value[:, kv].reshape(columns, head)
        score = lax.dot_general(q_rows, k, (((1,), (1,)), ((), ())), preferred_element_type=F32) * scale
        score = jnp.where(live, score, -1e30)
        top = jnp.max(score, axis=1, keepdims=True).astype(BF16).astype(F32)
        expo = jnp.where(live, jnp.exp(score - top), 0.0)
        total = jnp.sum(expo, axis=1, keepdims=True)
        summed = jnp.dot(expo.astype(BF16), v, preferred_element_type=F32)
        total_row = as_row(total)
        high = total_row.astype(BF16).astype(F32)
        stats = jnp.where(
            stat_row == 0, as_row(top), jnp.where(stat_row == 1, high, jnp.where(stat_row == 2, total_row - high, 0.0))
        )
        return summed.astype(BF16), stats.astype(BF16)

    summed, stats = attend(me, q_send[...])
    pay_all[me, 0:rows, :] = summed
    pay_all[me, rows : rows + 16, :] = stats

    def attend_step(i):
        from_peer(q_send, q_all, q_ss, q_rs, i).wait_recv()
        summed, stats = attend(peer(i), q_all[peer(i)])
        pay_send[i, 0:rows, :] = summed
        pay_send[i, rows : rows + 16, :] = stats
        to_peer(pay_send.at[i], pay_all, pay_ss, pay_rs, i).start()

    repeat(1, n, attend_step)
    repeat(1, n, lambda i: from_peer(pay_send.at[i], pay_all, pay_ss, pay_rs, i).wait_recv())

    stat = pay_all[:, rows : rows + 16, :].astype(F32)
    top = stat[:, 0, :]
    total = stat[:, 1, :] + stat[:, 2, :]
    factor = jnp.exp(top - jnp.max(top, axis=0, keepdims=True))
    share = factor / jnp.sum(factor * total, axis=0, keepdims=True)
    acc = jnp.zeros((rows, head), F32)
    for p in range(n):
        c = jnp.sum(jnp.where(eye, share[p : p + 1, :], 0.0), axis=1, keepdims=True)
        acc = acc + c * pay_all[p, 0:rows, :].astype(F32)
    att_send[...] = acc.astype(BF16)
    swap = to_pair(att_send, att_recv, 1)
    swap.start()

    def side_by_side(x):
        return jnp.concatenate([x[h * requests : (h + 1) * requests] for h in range(own)], axis=1)

    loads[2].wait()
    codes.wait()
    code = jnp.concatenate([code_own, code_recv[...]], axis=0)[:, 0:1]
    slot_of = lax.broadcasted_iota(jnp.int32, (2 * requests, slots * rank), 1) // rank
    picked = slot_of == code
    swap.wait()
    both = jnp.concatenate(
        [side_by_side(att_send[...].astype(F32)), side_by_side(att_recv[...].astype(F32))], axis=0
    ).astype(BF16)

    every = lax.dot_general(
        both, down[...].reshape(slots * rank, features), (((1,), (1,)), ((), ())), preferred_element_type=F32
    )
    every = jnp.where(picked, every, 0.0)
    part = every[:, 0:128]
    for j in range(1, slots * rank // 128):
        part = part + every[:, j * 128 : (j + 1) * 128]
    part = part + pltpu.roll(part, rank, 1)
    shr_send[...] = part
    shr_all[me] = part
    repeat(1, n, lambda i: to_peer(shr_send, shr_all, shr_ss, shr_rs, i).start())

    def base_step(i):
        w_copy(i).wait()
        base_send[i] = jnp.dot(both, weight[i], preferred_element_type=F32).astype(BF16)
        to_peer(base_send.at[i], base_all, base_ss, base_rs, i).start()

    repeat(1, n, base_step)
    w_copy(n).wait()
    base_all[me] = jnp.dot(both, weight[0], preferred_element_type=F32).astype(BF16)

    loads[3].wait()
    repeat(1, n, lambda i: from_peer(shr_send, shr_all, shr_ss, shr_rs, i).wait_recv())
    shrink = jnp.sum(shr_all[...], axis=0).astype(BF16).astype(F32)
    spread = jnp.concatenate([shrink] * (slots * rank // 128), axis=1)
    spread = jnp.where(picked, spread, 0.0).astype(BF16)
    expand = jnp.dot(spread, up[...].reshape(slots * rank, features), preferred_element_type=F32)
    fin_own[...] = expand[0:requests]
    fin_send[...] = expand[requests:]

    repeat(1, n, lambda i: from_peer(base_send.at[i], base_all, base_ss, base_rs, i).wait_recv())
    base = jnp.sum(base_all[...].astype(F32), axis=0)
    if split:
        half = pl.ds(pl.multiple_of(r * width, 128), width)
        fin_own[:, half] = fin_own[:, half] + base[0:requests]
        fin_send[:, half] = fin_send[:, half] + base[requests:]
    else:
        fin_own[...] = fin_own[...] + base[0:requests]
    last = to_pair(fin_send, fin_recv, 2)
    last.start()

    def drain(i):
        to_peer(q_send, q_all, q_ss, q_rs, i).wait_send()
        to_peer(pay_send.at[i], pay_all, pay_ss, pay_rs, i).wait_send()
        to_peer(shr_send, shr_all, shr_ss, shr_rs, i).wait_send()
        to_peer(base_send.at[i], base_all, base_ss, base_rs, i).wait_send()

    repeat(1, n, drain)
    last.wait()
    out[...] = (fin_own[...] + fin_recv[...]).astype(BF16)


def shards(n, query, key, value, length, weight, down, up, table, slot):
    requests, features = query.shape
    _, kv_heads, span, head = key.shape
    resident, rank, _ = down.shape
    slots = table.shape[0]
    rows = max(16, requests * (features // head))
    width = features // 2 if features % 256 == 0 else features
    smem = pl.BlockSpec(memory_space=pltpu.SMEM)
    vmem = pl.BlockSpec(memory_space=pltpu.VMEM)
    hbm = pl.BlockSpec(memory_space=pl.ANY)
    placed = jax.ShapeDtypeStruct((slots, rank, features), BF16)
    slot_down, slot_up = pl.pallas_call(
        gather_kernel,
        out_shape=(placed, placed),
        in_specs=[smem, hbm, hbm],
        out_specs=(hbm, hbm),
        scratch_shapes=[pltpu.SemaphoreType.DMA((2, slots))],
        name="gather_slots",
    )(table, down, up)
    dma = pltpu.SemaphoreType.DMA
    return pl.pallas_call(
        functools.partial(main_kernel, n, resident),
        out_shape=jax.ShapeDtypeStruct((requests, features), BF16),
        in_specs=[smem, smem, smem, vmem, hbm, hbm, hbm, hbm, hbm],
        out_specs=vmem,
        scratch_shapes=[
            pltpu.VMEM(key.shape, BF16),
            pltpu.VMEM(value.shape, BF16),
            pltpu.VMEM((n, features, width), BF16),
            pltpu.VMEM((slots, rank, features), BF16),
            pltpu.VMEM((slots, rank, features), BF16),
            pltpu.VMEM((rows, head), BF16),
            pltpu.VMEM((n, rows, head), BF16),
            pltpu.VMEM((n, rows + 16, head), BF16),
            pltpu.VMEM((n, rows + 16, head), BF16),
            pltpu.VMEM((rows, head), BF16),
            pltpu.VMEM((rows, head), BF16),
            pltpu.VMEM((requests, 128), jnp.int32),
            pltpu.VMEM((requests, 128), jnp.int32),
            pltpu.VMEM((2 * requests, 128), F32),
            pltpu.VMEM((n, 2 * requests, 128), F32),
            pltpu.VMEM((n, 2 * requests, width), BF16),
            pltpu.VMEM((n, 2 * requests, width), BF16),
            pltpu.VMEM((requests, features), F32),
            pltpu.VMEM((requests, features), F32),
            pltpu.VMEM((requests, features), F32),
            dma((4,)),
            dma((n,)),
            dma((n,)),
            dma((n,)),
            dma((n,)),
            dma((n,)),
            dma((n,)),
            dma((n,)),
            dma((n,)),
            dma((n,)),
            dma((3,)),
            dma((3,)),
        ],
        compiler_params=pltpu.CompilerParams(
            collective_id=0, has_side_effects=True, vmem_limit_bytes=48 * 1024 * 1024
        ),
        name="decode_block",
    )(length, slot, table, query, key, value, weight, slot_down, slot_up)


def solution(mesh):
    in_specs = (
        P(("groups", "replica"), "tensor"),
        P(("groups", "replica"), None, "tensor", None),
        P(("groups", "replica"), None, "tensor", None),
        P(("groups", "replica")),
        P("tensor", None),
        P("replica", None, "tensor"),
        P("replica", None, "tensor"),
        P("groups"),
        P(("groups", "replica")),
    )
    out_specs = P(("groups", "replica"), "tensor")
    body = functools.partial(shards, mesh.shape["tensor"])
    return jax.shard_map(body, mesh=mesh, in_specs=in_specs, out_specs=out_specs, check_vma=False)
```

time: 167 us -> 287 us (1.72)
  Pallas kernels: 0 us -> 284 us
  blocking collectives: 59 us -> 0 us
  waiting for transfers between devices: 21.1 us -> 0 us
  starting transfers between devices: 20.4 us -> 0 us
  local copies, waits for them, and re-layouts: 21.5 us -> 2.81 us
  other arithmetic: 15.3 us -> 0 us
  matrix products: 15 us -> 0 us
  between operations: 13.5 us -> 0.09 us
    pallas_call x0 -> x2, Pallas kernels: none -> 284 us  [the longest x1 257 us: shards(): pl.pallas_call(gather_kernel, out_shape=(placed, placed), in_specs=[smem,...]
    all_gather x1 -> x0, blocking collectives: 32.6 us -> none  [shards(): whole = lax.all_gather(query, 'tensor', axis=1, tiled=True)]
    all_to_all x4 -> x0, starting transfers between devices: 20.4 us -> none  [the longest x1 5.94 us: shards(): lax.all_to_all(summed[None].astype(jnp.bfloat16), 'tensor', split_axis=2,...]
    psum x1 -> x0, blocking collectives: 18.2 us -> none  [shards(): reduced_features = lax.psum(shrink_part, 'tensor').astype(jnp.bfloat16)]
    gather x2 -> x0, local copies, waits for them, and re-layouts: 17.1 us -> none  [the longest x1 8.55 us: shards(): adapter_up_weight[replica_slot_index]]
    dot_general x5 -> x0, matrix products: 15 us -> none  [the longest x1 8.8 us: shards(): jnp.dot(attention_output, output_weight, preferred_element_type=jnp.float32)]
    all_to_all x4 -> x0, waiting for transfers between devices: 10.6 us -> none  [the longest x1 6.93 us: shards(): lax.all_to_all(summed[None].astype(jnp.bfloat16), 'tensor', split_axis=2,...]
    reduce_scatter x1 -> x0, waiting for transfers between devices: 10.5 us -> none  [shards(): lax.psum_scatter(partial_value, 'tensor', scatter_dimension=1, tiled=True)]
  transfers between devices with their start and end apart: 5 -> 0, of which waited for: 3 -> 0; matrix products, arithmetic and copies ran while one was open for 23% -> 0% of each run, Pallas kernels for 0% -> 0%
where the time goes in v1:
time: 287 us
  Pallas kernels  284 us (99%)
    pallas_call x1, Pallas kernels, shards(): pl.pallas_call(gather_kernel, out_shape=(placed, placed), in_specs=[smem,...  257 us
    pallas_call x1, Pallas kernels, shards(): pl.pallas_call(functools.partial(main_kernel, n, resident), out_shape=jax...  27.4 us

profile of v1, /device:TPU:0, one launch (start us, length us, event | category | flops | bytes accessed | tf_op | source)
XLA Modules:
  0.0 286.8 jit_solution(15415708686058193099)
XLA Ops:
  0.0 0.0 copy-start.4
  0.0 0.0 copy-start.6
  0.0 0.0 copy-start.5
  0.0 0.0 copy-start.2
  0.0 0.0 copy-start.1
  0.0 0.0 copy-start.3
  0.0 256.6 %gather_slots.1 = (bf16[32,64,1024]{2,1,0:T(8,128)(2,1)}, bf16[32,64,1024]{2,1,0:T(8,128)(2,1)}) custom-call(s32[32]{0:T(128)} %table.3, bf16[128,64,1024]{2,1,0:T(8,128)(2,1)} %down.1, bf16[128,64,1024]{2,1,0:T(8,128)(2,1)} %up.1), custom_call_target="tpu_custom_call" | custom-call | tf_op jit(solution)/shard_map/gather_slots/pallas_call | solution.py:261
  256.6 0.0 copy-done.4
  256.6 0.0 copy-done.6
  256.6 0.0 copy-done.5
  256.7 0.0 copy-done.2
  256.7 0.0 copy-done.1
  256.7 0.0 copy-done.3
  256.7 0.0 copy-start
  256.7 2.2 copy-done
  258.9 27.4 %decode_block.1 = bf16[8,1024]{1,0:T(8,128)(2,1)S(1)} custom-call(s32[8]{0:T(128)S(1)} %copy-done.5, s32[8]{0:T(128)S(1)} %copy-done.6, s32[32]{0:T(128)S(1)} %copy-done.4, bf16[8,1024]{1,0:T(8,128)(2,1)S(1)} %copy-done.3, bf16[8,8,32,128]{3,2,1,0:T(8,128)(2,1)S(1)} %copy-done.1, bf16[8,8,32,128]{3,2,1,0:T(8,128)(2,1)S(1)} %copy-done.2, ...), custom_call_target="tpu_custom_call" | custom-call | tf_op jit(solution)/shard_map/decode_block/pallas_call | solution.py:270
  286.2 0.6 copy.11
Async XLA Ops:
  0.0 256.6 %copy-start.4 = (s32[32]{0:T(128)S(1)}, s32[32]{0:T(128)}, u32[]{:S(2)}) copy-start(s32[32]{0:T(128)} %table.3) | copy-start | bytes 388
  0.0 256.6 %copy-start.6 = (s32[8]{0:T(128)S(1)}, s32[8]{0:T(128)}, u32[]{:S(2)}) copy-start(s32[8]{0:T(128)} %slot.1) | copy-start | bytes 100
  0.0 256.6 %copy-start.5 = (s32[8]{0:T(128)S(1)}, s32[8]{0:T(128)}, u32[]{:S(2)}) copy-start(s32[8]{0:T(128)} %length.1) | copy-start | bytes 100
  0.0 256.7 %copy-start.2 = (bf16[8,8,32,128]{3,2,1,0:T(8,128)(2,1)S(1)}, bf16[8,8,32,128]{3,2,1,0:T(8,128)(2,1)}, u32[]{:S(2)}) copy-start(bf16[8,8,32,128]{3,2,1,0:T(8,128)(2,1)} %value_hbm.1) | copy-start | bytes 1572868
  0.0 256.7 %copy-start.1 = (bf16[8,8,32,128]{3,2,1,0:T(8,128)(2,1)S(1)}, bf16[8,8,32,128]{3,2,1,0:T(8,128)(2,1)}, u32[]{:S(2)}) copy-start(bf16[8,8,32,128]{3,2,1,0:T(8,128)(2,1)} %key_hbm.1) | copy-start | bytes 1572868
  0.0 256.7 %copy-start.3 = (bf16[8,1024]{1,0:T(8,128)(2,1)S(1)}, bf16[8,1024]{1,0:T(8,128)(2,1)}, u32[]{:S(2)}) copy-start(bf16[8,1024]{1,0:T(8,128)(2,1)} %query.1) | copy-start | bytes 49156
  256.7 2.2 copy-start

commit v2 on v1

--- a/solution.py
+++ b/solution.py
@@ -35,12 +35,12 @@
 
 def main_kernel(
     n, resident,
-    length, slot, table, query, key_hbm, value_hbm, weight_hbm, down_hbm, up_hbm,
+    length, slot, table, query, key, value, weight_hbm, down, up,
     out,
-    key, value, weight, down, up,
+    weight,
     q_send, q_all, pay_send, pay_all, att_send, att_recv, code_send, code_recv,
     shr_send, shr_all, base_send, base_all, fin_own, fin_send, fin_recv,
-    load_sem, w_sem, q_ss, q_rs, pay_ss, pay_rs, shr_ss, shr_rs, base_ss, base_rs, pair_ss, pair_rs,
+    w_sem, q_ss, q_rs, pay_ss, pay_rs, shr_ss, shr_rs, base_ss, base_rs, pair_ss, pair_rs,
 ):
     me = lax.axis_index("tensor")
     r = lax.axis_index("replica")
@@ -65,16 +65,7 @@
             weight_hbm.at[:, pl.ds(pl.multiple_of(start, 128), width)], weight.at[i % n], w_sem.at[i % n]
         )
 
-    loads = [
-        pltpu.make_async_copy(key_hbm, key, load_sem.at[0]),
-        pltpu.make_async_copy(value_hbm, value, load_sem.at[1]),
-        pltpu.make_async_copy(down_hbm, down, load_sem.at[2]),
-        pltpu.make_async_copy(up_hbm, up, load_sem.at[3]),
-    ]
-    for c in loads[:3]:
-        c.start()
     repeat(1, n + 1, lambda i: w_copy(i).start())
-    loads[3].start()
 
     barrier = pltpu.get_barrier_semaphore()
     repeat(1, n, lambda i: pl.semaphore_signal(barrier, inc=1, device_id={"tensor": peer(i)}, device_id_type=MESH))
@@ -131,9 +122,6 @@
     eye = lax.broadcasted_iota(jnp.int32, (rows, 128), 0) == lax.broadcasted_iota(jnp.int32, (rows, 128), 1)
     stat_row = lax.broadcasted_iota(jnp.int32, (16, 128), 0)
     scale = 1.0 / (float(head) ** 0.5)
-
-    loads[0].wait()
-    loads[1].wait()
 
     def as_row(c):
         return jnp.sum(jnp.where(eye, c, 0.0), axis=0, keepdims=True)
@@ -185,7 +173,6 @@
     def side_by_side(x):
         return jnp.concatenate([x[h * requests : (h + 1) * requests] for h in range(own)], axis=1)
 
-    loads[2].wait()
     codes.wait()
     code = jnp.concatenate([code_own, code_recv[...]], axis=0)[:, 0:1]
     slot_of = lax.broadcasted_iota(jnp.int32, (2 * requests, slots * rank), 1) // rank
@@ -216,7 +203,6 @@
     w_copy(n).wait()
     base_all[me] = jnp.dot(both, weight[0], preferred_element_type=F32).astype(BF16)
 
-    loads[3].wait()
     repeat(1, n, lambda i: from_peer(shr_send, shr_all, shr_ss, shr_rs, i).wait_recv())
     shrink = jnp.sum(shr_all[...], axis=0).astype(BF16).astype(F32)
     spread = jnp.concatenate([shrink] * (slots * rank // 128), axis=1)
@@ -262,22 +248,19 @@
         gather_kernel,
         out_shape=(placed, placed),
         in_specs=[smem, hbm, hbm],
-        out_specs=(hbm, hbm),
+        out_specs=(vmem, vmem),
         scratch_shapes=[pltpu.SemaphoreType.DMA((2, slots))],
+        compiler_params=pltpu.CompilerParams(vmem_limit_bytes=40 * 1024 * 1024),
         name="gather_slots",
     )(table, down, up)
     dma = pltpu.SemaphoreType.DMA
     return pl.pallas_call(
         functools.partial(main_kernel, n, resident),
         out_shape=jax.ShapeDtypeStruct((requests, features), BF16),
-        in_specs=[smem, smem, smem, vmem, hbm, hbm, hbm, hbm, hbm],
+        in_specs=[smem, smem, smem, vmem, vmem, vmem, hbm, vmem, vmem],
         out_specs=vmem,
         scratch_shapes=[
-            pltpu.VMEM(key.shape, BF16),
-            pltpu.VMEM(value.shape, BF16),
             pltpu.VMEM((n, features, width), BF16),
-            pltpu.VMEM((slots, rank, features), BF16),
-            pltpu.VMEM((slots, rank, features), BF16),
             pltpu.VMEM((rows, head), BF16),
             pltpu.VMEM((n, rows, head), BF16),
             pltpu.VMEM((n, rows + 16, head), BF16),
@@ -293,7 +276,6 @@
             pltpu.VMEM((requests, features), F32),
             pltpu.VMEM((requests, features), F32),
             pltpu.VMEM((requests, features), F32),
-            dma((4,)),
             dma((n,)),
             dma((n,)),
             dma((n,)),
@@ -307,7 +289,7 @@
             dma((3,)),
         ],
         compiler_params=pltpu.CompilerParams(
-            collective_id=0, has_side_effects=True, vmem_limit_bytes=48 * 1024 * 1024
+            collective_id=0, has_side_effects=True, vmem_limit_bytes=40 * 1024 * 1024
         ),
         name="decode_block",
     )(length, slot, table, query, key, value, weight, slot_down, slot_up)

time: 287 us -> 33.3 us (0.12)
  Pallas kernels: 284 us -> 31.8 us
    pallas_call x1, Pallas kernels: 257 us -> 4.8 us  [shards(): pl.pallas_call(gather_kernel, out_shape=(placed, placed), in_specs=[smem,...]
where the time goes in v2:
time: 33.3 us; the launch traced here: 33.2 us
  Pallas kernels  31.8 us (95%)
  local copies, waits for them, and re-layouts  1.37 us (4%)
    pallas_call x1, Pallas kernels, shards(): pl.pallas_call(functools.partial(main_kernel, n, resident), out_shape=jax...  27 us
    pallas_call x1, Pallas kernels, shards(): pl.pallas_call(gather_kernel, out_shape=(placed, placed), in_specs=[smem,...  4.8 us
    unnamed x13, local copies, waits for them, and re-layouts  1.37 us

profile of v2, /device:TPU:0, one launch (start us, length us, event | category | flops | bytes accessed | tf_op | source)
XLA Modules:
  0.0 33.2 jit_solution(13751720399932232191)
XLA Ops:
  0.0 0.0 copy-start.1
  0.0 0.0 copy-start
  0.0 0.0 copy-start.3
  0.0 0.7 %copy-done.3 = s32[32]{0:T(128)S(1)} copy-done((s32[32]{0:T(128)S(1)}, s32[32]{0:T(128)}, u32[]{:S(2)}) %copy-start.3) | copy-done | bytes 152
  0.7 0.0 copy-start.2
  0.8 0.0 copy-start.4
  0.8 0.0 copy-start.5
  0.8 4.8 %gather_slots.1 = (bf16[32,64,1024]{2,1,0:T(8,128)(2,1)S(1)}, bf16[32,64,1024]{2,1,0:T(8,128)(2,1)S(1)}) custom-call(s32[32]{0:T(128)S(1)} %copy-done.3, bf16[128,64,1024]{2,1,0:T(8,128)(2,1)} %down.1, bf16[128,64,1024]{2,1,0:T(8,128)(2,1)} %up.1), custom_call_target="tpu_custom_call" | custom-call | tf_op jit(solution)/shard_map/gather_slots/pallas_call | solution.py:247
  5.6 0.0 copy-done.1
  5.6 0.0 copy-done
  5.6 0.0 copy-done.2
  5.6 0.0 copy-done.4
  5.6 0.0 copy-done.5
  5.6 27.0 %decode_block.1 = bf16[8,1024]{1,0:T(8,128)(2,1)S(1)} custom-call(s32[8]{0:T(128)S(1)} %copy-done.4, s32[8]{0:T(128)S(1)} %copy-done.5, s32[32]{0:T(128)S(1)} %copy-done.3, bf16[8,1024]{1,0:T(8,128)(2,1)S(1)} %copy-done.2, bf16[8,8,32,128]{3,2,1,0:T(8,128)(2,1)S(1)} %copy-done, bf16[8,8,32,128]{3,2,1,0:T(8,128)(2,1)S(1)} %copy-done.1, ...), custom_call_target="tpu_custom_call" | custom-call | tf_op jit(solution)/shard_map/decode_block/pallas_call | solution.py:257
  32.6 0.6 %copy.11 = bf16[8,1024]{1,0:T(8,128)(2,1)} copy(bf16[8,1024]{1,0:T(8,128)(2,1)S(1)} %decode_block.1) | data formatting | bytes 32768
Async XLA Ops:
  0.0 5.6 %copy-start.1 = (bf16[8,8,32,128]{3,2,1,0:T(8,128)(2,1)S(1)}, bf16[8,8,32,128]{3,2,1,0:T(8,128)(2,1)}, u32[]{:S(2)}) copy-start(bf16[8,8,32,128]{3,2,1,0:T(8,128)(2,1)} %value.1) | copy-start | bytes 1572868
  0.0 5.6 %copy-start = (bf16[8,8,32,128]{3,2,1,0:T(8,128)(2,1)S(1)}, bf16[8,8,32,128]{3,2,1,0:T(8,128)(2,1)}, u32[]{:S(2)}) copy-start(bf16[8,8,32,128]{3,2,1,0:T(8,128)(2,1)} %key.1) | copy-start | bytes 1572868
  0.0 0.7 %copy-start.3 = (s32[32]{0:T(128)S(1)}, s32[32]{0:T(128)}, u32[]{:S(2)}) copy-start(s32[32]{0:T(128)} %table.3) | copy-start | bytes 388
  0.7 4.8 %copy-start.2 = (bf16[8,1024]{1,0:T(8,128)(2,1)S(1)}, bf16[8,1024]{1,0:T(8,128)(2,1)}, u32[]{:S(2)}) copy-start(bf16[8,1024]{1,0:T(8,128)(2,1)} %query.1) | copy-start | bytes 49156
  0.8 4.8 %copy-start.4 = (s32[8]{0:T(128)S(1)}, s32[8]{0:T(128)}, u32[]{:S(2)}) copy-start(s32[8]{0:T(128)} %length.1) | copy-start | bytes 100
  0.8 4.9 %copy-start.5 = (s32[8]{0:T(128)S(1)}, s32[8]{0:T(128)}, u32[]{:S(2)}) copy-start(s32[8]{0:T(128)} %slot.1) | copy-start | bytes 100

commit v3 on v2

--- a/solution.py
+++ b/solution.py
@@ -22,15 +22,39 @@
 
 def gather_kernel(table, down, up, out_down, out_up, sems):
     resident = down.shape[0]
-    copies = []
-    for s in range(out_down.shape[0]):
+    r = lax.axis_index("replica")
+    slots = out_down.shape[0]
+
+    def copies(s):
         index = lax.rem(table[s], resident)
-        copies.append(pltpu.make_async_copy(down.at[index], out_down.at[s], sems.at[0, s]))
-        copies.append(pltpu.make_async_copy(up.at[index], out_up.at[s], sems.at[1, s]))
-    for c in copies:
-        c.start()
-    for c in copies:
-        c.wait()
+        return (
+            pltpu.make_async_copy(down.at[index], out_down.at[s], sems.at[0, s]),
+            pltpu.make_async_copy(up.at[index], out_up.at[s], sems.at[1, s]),
+        )
+
+    def at_home(s):
+        return table[s] // resident == r
+
+    for s in range(slots):
+
+        @pl.when(at_home(s))
+        def _():
+            for c in copies(s):
+                c.start()
+
+    for s in range(slots):
+
+        @pl.when(jnp.logical_not(at_home(s)))
+        def _():
+            out_down[s] = jnp.zeros(out_down.shape[1:], out_down.dtype)
+            out_up[s] = jnp.zeros(out_up.shape[1:], out_up.dtype)
+
+    for s in range(slots):
+
+        @pl.when(at_home(s))
+        def _():
+            for c in copies(s):
+                c.wait()
 
 
 def main_kernel(

time: 33.3 us -> 32 us (0.961)
  Pallas kernels: 31.8 us -> 30.4 us
    pallas_call x1, Pallas kernels: 4.8 us -> 3.72 us  [shards(): pl.pallas_call(gather_kernel, out_shape=(placed, placed), in_specs=[smem,...]
where the time goes in v3:
time: 32 us; the launch traced here: 31.8 us
  Pallas kernels  30.4 us (95%)
  local copies, waits for them, and re-layouts  1.37 us (4%)
    pallas_call x1, Pallas kernels, shards(): pl.pallas_call(functools.partial(main_kernel, n, resident), out_shape=jax...  26.6 us
    pallas_call x1, Pallas kernels, shards(): pl.pallas_call(gather_kernel, out_shape=(placed, placed), in_specs=[smem,...  3.72 us
    unnamed x13, local copies, waits for them, and re-layouts  1.37 us

profile of v3, /device:TPU:0, one launch (start us, length us, event | category | flops | bytes accessed | tf_op | source)
XLA Modules:
  0.0 31.8 jit_solution(11782208487989106866)
XLA Ops:
  0.0 0.0 copy-start.1
  0.0 0.0 copy-start
  0.0 0.0 copy-start.3
  0.0 0.7 %copy-done.3 = s32[32]{0:T(128)S(1)} copy-done((s32[32]{0:T(128)S(1)}, s32[32]{0:T(128)}, u32[]{:S(2)}) %copy-start.3) | copy-done | bytes 152
  0.7 0.0 copy-start.2
  0.8 0.0 copy-start.4
  0.8 0.0 copy-start.5
  0.8 3.7 %gather_slots.1 = (bf16[32,64,1024]{2,1,0:T(8,128)(2,1)S(1)}, bf16[32,64,1024]{2,1,0:T(8,128)(2,1)S(1)}) custom-call(s32[32]{0:T(128)S(1)} %copy-done.3, bf16[128,64,1024]{2,1,0:T(8,128)(2,1)} %down.1, bf16[128,64,1024]{2,1,0:T(8,128)(2,1)} %up.1), custom_call_target="tpu_custom_call" | custom-call | tf_op jit(solution)/shard_map/gather_slots/pallas_call | solution.py:271
  4.5 0.0 copy-done.1
  4.5 0.0 copy-done
  4.5 0.0 copy-done.2
  4.5 0.0 copy-done.4
  4.5 0.0 copy-done.5
  4.5 26.6 %decode_block.1 = bf16[8,1024]{1,0:T(8,128)(2,1)S(1)} custom-call(s32[8]{0:T(128)S(1)} %copy-done.4, s32[8]{0:T(128)S(1)} %copy-done.5, s32[32]{0:T(128)S(1)} %copy-done.3, bf16[8,1024]{1,0:T(8,128)(2,1)S(1)} %copy-done.2, bf16[8,8,32,128]{3,2,1,0:T(8,128)(2,1)S(1)} %copy-done, bf16[8,8,32,128]{3,2,1,0:T(8,128)(2,1)S(1)} %copy-done.1, ...), custom_call_target="tpu_custom_call" | custom-call | tf_op jit(solution)/shard_map/decode_block/pallas_call | solution.py:281
  31.2 0.6 %copy.11 = bf16[8,1024]{1,0:T(8,128)(2,1)} copy(bf16[8,1024]{1,0:T(8,128)(2,1)S(1)} %decode_block.1) | data formatting | bytes 32768
Async XLA Ops:
  0.0 4.5 %copy-start.1 = (bf16[8,8,32,128]{3,2,1,0:T(8,128)(2,1)S(1)}, bf16[8,8,32,128]{3,2,1,0:T(8,128)(2,1)}, u32[]{:S(2)}) copy-start(bf16[8,8,32,128]{3,2,1,0:T(8,128)(2,1)} %value.1) | copy-start | bytes 1572868
  0.0 4.5 %copy-start = (bf16[8,8,32,128]{3,2,1,0:T(8,128)(2,1)S(1)}, bf16[8,8,32,128]{3,2,1,0:T(8,128)(2,1)}, u32[]{:S(2)}) copy-start(bf16[8,8,32,128]{3,2,1,0:T(8,128)(2,1)} %key.1) | copy-start | bytes 1572868
  0.0 0.7 %copy-start.3 = (s32[32]{0:T(128)S(1)}, s32[32]{0:T(128)}, u32[]{:S(2)}) copy-start(s32[32]{0:T(128)} %table.3) | copy-start | bytes 388
  0.7 3.8 %copy-start.2 = (bf16[8,1024]{1,0:T(8,128)(2,1)S(1)}, bf16[8,1024]{1,0:T(8,128)(2,1)}, u32[]{:S(2)}) copy-start(bf16[8,1024]{1,0:T(8,128)(2,1)} %query.1) | copy-start | bytes 49156
  0.8 3.8 %copy-start.4 = (s32[8]{0:T(128)S(1)}, s32[8]{0:T(128)}, u32[]{:S(2)}) copy-start(s32[8]{0:T(128)} %length.1) | copy-start | bytes 100
  0.8 3.8 %copy-start.5 = (s32[8]{0:T(128)S(1)}, s32[8]{0:T(128)}, u32[]{:S(2)}) copy-start(s32[8]{0:T(128)} %slot.1) | copy-start | bytes 100

commit v4 on v3

--- a/solution.py
+++ b/solution.py
@@ -80,7 +80,14 @@
     rank = down.shape[1]
 
     def peer(i):
-        return lax.rem(me + i, n)
+        if n & (n - 1):
+            return (me + i) % n
+        step = i % n
+        other, bit = 0, 1
+        while bit < n:
+            other = other + bit * ((me // bit + step // bit) % 2)
+            bit *= 2
+        return other
 
     def w_copy(i):
         p = peer(i)
@@ -214,6 +221,9 @@
     for j in range(1, slots * rank // 128):
         part = part + every[:, j * 128 : (j + 1) * 128]
     part = part + pltpu.roll(part, rank, 1)
+    high = part.astype(BF16).astype(F32)
+    lane = lax.broadcasted_iota(jnp.int32, part.shape, 1)
+    part = jnp.where(lane < rank, high, part - high).astype(BF16)
     shr_send[...] = part
     shr_all[me] = part
     repeat(1, n, lambda i: to_peer(shr_send, shr_all, shr_ss, shr_rs, i).start())
@@ -228,7 +238,8 @@
     base_all[me] = jnp.dot(both, weight[0], preferred_element_type=F32).astype(BF16)
 
     repeat(1, n, lambda i: from_peer(shr_send, shr_all, shr_ss, shr_rs, i).wait_recv())
-    shrink = jnp.sum(shr_all[...], axis=0).astype(BF16).astype(F32)
+    shrink = jnp.sum(shr_all[...].astype(F32), axis=0)
+    shrink = (shrink + pltpu.roll(shrink, rank, 1)).astype(BF16).astype(F32)
     spread = jnp.concatenate([shrink] * (slots * rank // 128), axis=1)
     spread = jnp.where(picked, spread, 0.0).astype(BF16)
     expand = jnp.dot(spread, up[...].reshape(slots * rank, features), preferred_element_type=F32)
@@ -293,8 +304,8 @@
             pltpu.VMEM((rows, head), BF16),
             pltpu.VMEM((requests, 128), jnp.int32),
             pltpu.VMEM((requests, 128), jnp.int32),
-            pltpu.VMEM((2 * requests, 128), F32),
-            pltpu.VMEM((n, 2 * requests, 128), F32),
+            pltpu.VMEM((2 * requests, 128), BF16),
+            pltpu.VMEM((n, 2 * requests, 128), BF16),
             pltpu.VMEM((n, 2 * requests, width), BF16),
             pltpu.VMEM((n, 2 * requests, width), BF16),
             pltpu.VMEM((requests, features), F32),

time: 32 us -> 31.4 us (0.981)
  Pallas kernels: 30.4 us -> 30 us
    pallas_call x1, Pallas kernels: 3.72 us -> 3.18 us  [shards(): pl.pallas_call(gather_kernel, out_shape=(placed, placed), in_specs=[smem,...]
where the time goes in v4:
time: 31.4 us
  Pallas kernels  30 us (96%)
  local copies, waits for them, and re-layouts  1.37 us (4%)
    pallas_call x1, Pallas kernels, shards(): pl.pallas_call(functools.partial(main_kernel, n, resident), out_shape=jax...  26.8 us
    pallas_call x1, Pallas kernels, shards(): pl.pallas_call(gather_kernel, out_shape=(placed, placed), in_specs=[smem,...  3.18 us
    unnamed x13, local copies, waits for them, and re-layouts  1.37 us

profile of v4, /device:TPU:0, one launch (start us, length us, event | category | flops | bytes accessed | tf_op | source)
XLA Modules:
  0.0 31.4 jit_solution(12658641452728301899)
XLA Ops:
  0.0 0.0 copy-start.1
  0.0 0.0 copy-start
  0.0 0.0 copy-start.3
  0.0 0.7 %copy-done.3 = s32[32]{0:T(128)S(1)} copy-done((s32[32]{0:T(128)S(1)}, s32[32]{0:T(128)}, u32[]{:S(2)}) %copy-start.3) | copy-done | bytes 152
  0.7 0.0 copy-start.2
  0.8 0.0 copy-start.4
  0.8 0.0 copy-start.5
  0.8 3.2 %gather_slots.1 = (bf16[32,64,1024]{2,1,0:T(8,128)(2,1)S(1)}, bf16[32,64,1024]{2,1,0:T(8,128)(2,1)S(1)}) custom-call(s32[32]{0:T(128)S(1)} %copy-done.3, bf16[128,64,1024]{2,1,0:T(8,128)(2,1)} %down.1, bf16[128,64,1024]{2,1,0:T(8,128)(2,1)} %up.1), custom_call_target="tpu_custom_call" | custom-call | tf_op jit(solution)/shard_map/gather_slots/pallas_call | solution.py:282
  3.9 0.0 copy-done.1
  4.0 0.0 copy-done
  4.0 0.0 copy-done.2
  4.0 0.0 copy-done.4
  4.0 0.0 copy-done.5
  4.0 26.8 %decode_block.1 = bf16[8,1024]{1,0:T(8,128)(2,1)S(1)} custom-call(s32[8]{0:T(128)S(1)} %copy-done.4, s32[8]{0:T(128)S(1)} %copy-done.5, s32[32]{0:T(128)S(1)} %copy-done.3, bf16[8,1024]{1,0:T(8,128)(2,1)S(1)} %copy-done.2, bf16[8,8,32,128]{3,2,1,0:T(8,128)(2,1)S(1)} %copy-done, bf16[8,8,32,128]{3,2,1,0:T(8,128)(2,1)S(1)} %copy-done.1, ...), custom_call_target="tpu_custom_call" | custom-call | tf_op jit(solution)/shard_map/decode_block/pallas_call | solution.py:292
  30.8 0.6 %copy.11 = bf16[8,1024]{1,0:T(8,128)(2,1)} copy(bf16[8,1024]{1,0:T(8,128)(2,1)S(1)} %decode_block.1) | data formatting | bytes 32768
Async XLA Ops:
  0.0 3.9 %copy-start.1 = (bf16[8,8,32,128]{3,2,1,0:T(8,128)(2,1)S(1)}, bf16[8,8,32,128]{3,2,1,0:T(8,128)(2,1)}, u32[]{:S(2)}) copy-start(bf16[8,8,32,128]{3,2,1,0:T(8,128)(2,1)} %value.1) | copy-start | bytes 1572868
  0.0 4.0 %copy-start = (bf16[8,8,32,128]{3,2,1,0:T(8,128)(2,1)S(1)}, bf16[8,8,32,128]{3,2,1,0:T(8,128)(2,1)}, u32[]{:S(2)}) copy-start(bf16[8,8,32,128]{3,2,1,0:T(8,128)(2,1)} %key.1) | copy-start | bytes 1572868
  0.0 0.7 %copy-start.3 = (s32[32]{0:T(128)S(1)}, s32[32]{0:T(128)}, u32[]{:S(2)}) copy-start(s32[32]{0:T(128)} %table.3) | copy-start | bytes 388
  0.7 3.2 %copy-start.2 = (bf16[8,1024]{1,0:T(8,128)(2,1)S(1)}, bf16[8,1024]{1,0:T(8,128)(2,1)}, u32[]{:S(2)}) copy-start(bf16[8,1024]{1,0:T(8,128)(2,1)} %query.1) | copy-start | bytes 49156
  0.8 3.2 %copy-start.4 = (s32[8]{0:T(128)S(1)}, s32[8]{0:T(128)}, u32[]{:S(2)}) copy-start(s32[8]{0:T(128)} %length.1) | copy-start | bytes 100
  0.8 3.2 %copy-start.5 = (s32[8]{0:T(128)S(1)}, s32[8]{0:T(128)}, u32[]{:S(2)}) copy-start(s32[8]{0:T(128)} %slot.1) | copy-start | bytes 100

commit v5 on v4

--- a/solution.py
+++ b/solution.py
@@ -96,7 +96,6 @@
             weight_hbm.at[:, pl.ds(pl.multiple_of(start, 128), width)], weight.at[i % n], w_sem.at[i % n]
         )
 
-    repeat(1, n + 1, lambda i: w_copy(i).start())
 
     barrier = pltpu.get_barrier_semaphore()
     repeat(1, n, lambda i: pl.semaphore_signal(barrier, inc=1, device_id={"tensor": peer(i)}, device_id_type=MESH))
@@ -142,6 +141,7 @@
     repeat(1, n, lambda i: to_peer(q_send, q_all, q_ss, q_rs, i).start())
     codes = to_pair(code_send, code_recv, 0)
     codes.start()
+    repeat(1, n + 1, lambda i: w_copy(i).start())
 
     columns = requests * span
     col = lax.broadcasted_iota(jnp.int32, (rows, columns), 1)

time: 31.4 us -> 31.2 us (level)
    pallas_call x1, Pallas kernels: 26.8 us -> 26 us  [shards(): pl.pallas_call(functools.partial(main_kernel, n, resident), out_shape=jax...]
    pallas_call x1, Pallas kernels: 3.18 us -> 3.78 us  [shards(): pl.pallas_call(gather_kernel, out_shape=(placed, placed), in_specs=[smem,...]
where the time goes in v5:
time: 31.2 us
  Pallas kernels  29.7 us (95%)
  local copies, waits for them, and re-layouts  1.37 us (4%)
    pallas_call x1, Pallas kernels, shards(): pl.pallas_call(functools.partial(main_kernel, n, resident), out_shape=jax...  26 us
    pallas_call x1, Pallas kernels, shards(): pl.pallas_call(gather_kernel, out_shape=(placed, placed), in_specs=[smem,...  3.78 us
    unnamed x13, local copies, waits for them, and re-layouts  1.37 us

profile of v5, /device:TPU:0, one launch (start us, length us, event | category | flops | bytes accessed | tf_op | source)
XLA Modules:
  0.0 31.2 jit_solution(15440703890254101099)
XLA Ops:
  0.0 0.0 copy-start.1
  0.0 0.0 copy-start
  0.0 0.0 copy-start.3
  0.0 0.7 %copy-done.3 = s32[32]{0:T(128)S(1)} copy-done((s32[32]{0:T(128)S(1)}, s32[32]{0:T(128)}, u32[]{:S(2)}) %copy-start.3) | copy-done | bytes 152
  0.7 0.0 copy-start.2
  0.8 0.0 copy-start.4
  0.8 0.0 copy-start.5
  0.8 3.8 %gather_slots.1 = (bf16[32,64,1024]{2,1,0:T(8,128)(2,1)S(1)}, bf16[32,64,1024]{2,1,0:T(8,128)(2,1)S(1)}) custom-call(s32[32]{0:T(128)S(1)} %copy-done.3, bf16[128,64,1024]{2,1,0:T(8,128)(2,1)} %down.1, bf16[128,64,1024]{2,1,0:T(8,128)(2,1)} %up.1), custom_call_target="tpu_custom_call" | custom-call | tf_op jit(solution)/shard_map/gather_slots/pallas_call | solution.py:282
  4.5 0.0 copy-done.1
  4.6 0.0 copy-done
  4.6 0.0 copy-done.2
  4.6 0.0 copy-done.4
  4.6 0.0 copy-done.5
  4.6 26.0 %decode_block.1 = bf16[8,1024]{1,0:T(8,128)(2,1)S(1)} custom-call(s32[8]{0:T(128)S(1)} %copy-done.4, s32[8]{0:T(128)S(1)} %copy-done.5, s32[32]{0:T(128)S(1)} %copy-done.3, bf16[8,1024]{1,0:T(8,128)(2,1)S(1)} %copy-done.2, bf16[8,8,32,128]{3,2,1,0:T(8,128)(2,1)S(1)} %copy-done, bf16[8,8,32,128]{3,2,1,0:T(8,128)(2,1)S(1)} %copy-done.1, ...), custom_call_target="tpu_custom_call" | custom-call | tf_op jit(solution)/shard_map/decode_block/pallas_call | solution.py:292
  30.6 0.6 %copy.11 = bf16[8,1024]{1,0:T(8,128)(2,1)} copy(bf16[8,1024]{1,0:T(8,128)(2,1)S(1)} %decode_block.1) | data formatting | bytes 32768
Async XLA Ops:
  0.0 4.5 %copy-start.1 = (bf16[8,8,32,128]{3,2,1,0:T(8,128)(2,1)S(1)}, bf16[8,8,32,128]{3,2,1,0:T(8,128)(2,1)}, u32[]{:S(2)}) copy-start(bf16[8,8,32,128]{3,2,1,0:T(8,128)(2,1)} %value.1) | copy-start | bytes 1572868
  0.0 4.6 %copy-start = (bf16[8,8,32,128]{3,2,1,0:T(8,128)(2,1)S(1)}, bf16[8,8,32,128]{3,2,1,0:T(8,128)(2,1)}, u32[]{:S(2)}) copy-start(bf16[8,8,32,128]{3,2,1,0:T(8,128)(2,1)} %key.1) | copy-start | bytes 1572868
  0.0 0.7 %copy-start.3 = (s32[32]{0:T(128)S(1)}, s32[32]{0:T(128)}, u32[]{:S(2)}) copy-start(s32[32]{0:T(128)} %table.3) | copy-start | bytes 388
  0.7 3.8 %copy-start.2 = (bf16[8,1024]{1,0:T(8,128)(2,1)S(1)}, bf16[8,1024]{1,0:T(8,128)(2,1)}, u32[]{:S(2)}) copy-start(bf16[8,1024]{1,0:T(8,128)(2,1)} %query.1) | copy-start | bytes 49156
  0.8 3.8 %copy-start.4 = (s32[8]{0:T(128)S(1)}, s32[8]{0:T(128)}, u32[]{:S(2)}) copy-start(s32[8]{0:T(128)} %length.1) | copy-start | bytes 100
  0.8 3.8 %copy-start.5 = (s32[8]{0:T(128)S(1)}, s32[8]{0:T(128)}, u32[]{:S(2)}) copy-start(s32[8]{0:T(128)} %slot.1) | copy-start | bytes 100
